TPU v7x, 32 devices: a whole 2x2x4 slice. The times are simulated.
32 devices in a mesh: tm: 4 (over y, x), stat: 8 (over z, core).
Axes of the slice: x: 2, y: 2, z: 4, core: 2. Of those that a mesh axis runs over, the one named last changes fastest.
Arguments:
- voltages: bfloat16 [512, 163840], P('stat', 'tm'), may hold values from -6 to 6
- taper: float32 [16, 4096], replicated, may hold values from -1.5 to 1.5
Outputs:
- visibility: float32 [4, 2, 512, 5, 64, 512], P('tm', None, 'stat')
All inputs are finite; a program needn't handle non-finite values.
Results may differ from a plain program's by a relative error of at most 0.0039.
Values may be sent and summed in bfloat16 or wider, within the bound.
A program may use at most 512 MiB of HBM per device.

v0:
```python
import math
import jax
import jax.numpy as jnp
from jax import lax
from jax.sharding import PartitionSpec as P

NSPEC = 25


def from_behind(value, axis, steps):
    count = lax.axis_size(axis)
    pairs = [(source, (source + steps) % count) for source in range(count)]
    return lax.ppermute(value, axis, pairs)


def dft_table(segment, channel_count, frame_len):
    sample_idx = jnp.arange(segment, dtype=jnp.int32)[:, None]
    channel_idx = jnp.arange(channel_count, dtype=jnp.int32)[None, :]
    angles = 2.0 * math.pi / segment * (sample_idx * channel_idx % segment).astype(jnp.float32)
    cosine = jnp.cos(angles)
    sine_part = jnp.sin(angles)
    upper = jnp.concatenate([cosine, -sine_part], axis=1)
    lower = jnp.concatenate([sine_part, cosine], axis=1)
    return jnp.concatenate([upper, lower], axis=0) / math.sqrt(frame_len)


def fold_twiddle(filtered, residue, tm_count, frame_len):
    row_count = filtered.shape[0]
    segment = frame_len // tm_count
    pieces = filtered.reshape(row_count, tm_count, segment)
    outer_idx = jnp.arange(tm_count, dtype=jnp.int32)
    outer_angles = 2.0 * math.pi / tm_count * (residue * outer_idx % tm_count).astype(jnp.float32)
    sum_real = jnp.sum(pieces * jnp.cos(outer_angles)[None, :, None], axis=1)
    sum_imag = -jnp.sum(pieces * jnp.sin(outer_angles)[None, :, None], axis=1)
    inner_idx = jnp.arange(segment, dtype=jnp.int32)
    inner_angles = 2.0 * math.pi / frame_len * (residue * inner_idx % frame_len).astype(jnp.float32)
    inner_cos = jnp.cos(inner_angles)[None, :]
    inner_sin = jnp.sin(inner_angles)[None, :]
    twisted_real = sum_real * inner_cos + sum_imag * inner_sin
    twisted_imag = sum_imag * inner_cos - sum_real * inner_sin
    return jnp.concatenate([twisted_real, twisted_imag], axis=1)


def polyphase(series, taper, spectra_count):
    row_count = series.shape[0]
    tap_count = taper.shape[0]
    frame_len = taper.shape[1]
    frames = series.reshape(row_count, spectra_count + tap_count - 1, frame_len)
    filtered = jnp.zeros((row_count, spectra_count, frame_len), jnp.float32)
    for tap_index in range(tap_count):
        filtered = filtered + taper[tap_index][None, None, :] * frames[
            :, tap_index : tap_index + spectra_count, :
        ].astype(jnp.float32)
    return filtered.reshape(row_count * spectra_count, frame_len)


def correlate(conjugated, partner_block, spectra_count):
    cross = jnp.einsum(
        "opisc,pmsc->oimc", conjugated, partner_block, preferred_element_type=jnp.float32
    )
    return cross / spectra_count


def shards(voltages, taper):
    tm_count = lax.axis_size("tm")
    stat_count = lax.axis_size("stat")
    tm_index = lax.axis_index("tm")
    local_inputs = voltages.shape[0]
    frame_len = taper.shape[1]
    segment = frame_len // tm_count
    channel_count = frame_len // 2 // tm_count
    spectra_count = NSPEC
    lag_count = stat_count // 2 + 1
    table = dft_table(segment, channel_count, frame_len)
    whole_series = lax.all_gather(voltages, "tm", axis=1, tiled=True)
    filtered = polyphase(whole_series, taper, spectra_count)
    twisted = fold_twiddle(filtered, tm_index, tm_count, frame_len)
    spectra = jnp.dot(
        twisted, table, precision=lax.Precision.HIGHEST, preferred_element_type=jnp.float32
    )
    spectra = spectra.reshape(local_inputs, spectra_count, 2, channel_count)
    own_block = jnp.transpose(spectra, (2, 0, 1, 3)).astype(jnp.bfloat16)
    conjugated = jnp.stack([own_block, jnp.stack([own_block[1], -own_block[0]])])
    visibility = jnp.zeros((2, local_inputs, lag_count, local_inputs, channel_count), jnp.float32)
    visibility = visibility.at[:, :, 0].set(correlate(conjugated, own_block, spectra_count))

    def lag_step(lag_index, carried):
        partner_block, accumulated = carried
        partner_block = from_behind(partner_block, "stat", -1)
        cross = correlate(conjugated, partner_block, spectra_count)
        accumulated = lax.dynamic_update_slice_in_dim(accumulated, cross[:, :, None], lag_index, 2)
        return (partner_block, accumulated)

    carried_out = lax.fori_loop(1, lag_count, lag_step, (own_block, visibility))
    visibility = carried_out[1]
    return visibility[None]


def solution(mesh):
    return jax.shard_map(
        shards,
        mesh=mesh,
        in_specs=(P("stat", "tm"), P()),
        out_specs=P("tm", None, "stat", None, None, None),
        check_vma=False,
    )
```

profile of v0, /device:TPU:0, one launch (start us, length us, event | category | flops | bytes accessed | tf_op | source)
XLA Modules:
  0.0 1070.2 jit_solution(5715505198837523400)
XLA Ops:
  26.6 178.4 %all-gather.2.cloned.1.call-done = bf16[64,163840]{1,0:T(8,128)(2,1)} async-done(((bf16[64,40960]{1,0:T(8,128)(2,1)}), bf16[64,163840]{1,0:T(8,128)(2,1)}) %all-gather.2.cloned.1.call-update) | async-done | bytes 20971536 | tf_op jit(solution)/shard_map/all_gather | solution.py:75
  205.0 22.7 %copy.22 = bf16[8,8,40,4096]{3,2,1,0:T(8,128)(2,1)} copy(bf16[8,8,40,4096]{3,1,2,0:T(8,128)(2,1)} %bitcast.68) | data formatting | bytes 41943040
  227.7 134.3 %multiply_add_fusion = f32[64,25,4096]{2,1,0:T(8,128)} fusion(bf16[64,40,4096]{2,1,0:T(8,128)(2,1)} %bitcast.66, f32[4096]{0:T(1024)S(1)} %bitcast.83, f32[4096]{0:T(1024)S(1)} %bitcast.84, f32[4096]{0:T(1024)S(1)} %bitcast.70, f32[4096]{0:T(1024)S(1)} %bitcast.71, f32[4096]{0:T(1024)S(1)} %bitcast.72, f32[4096]{0:T(1024)S(1)} %bitcast.73, ...), kind=kLoop, calls=%fused_computation.4 | loop fusion | flops 308019200 | bytes 236191744 | tf_op jit(solution)/shard_map/add | solution.py:51
  362.0 31.6 %reshape_reshape.3 = f32[1600,4,1024]{2,1,0:T(4,128)} reshape(f32[64,25,4096]{2,1,0:T(8,128)} %multiply_add_fusion) | data formatting | bytes 52428800 | tf_op jit(solution)/shard_map/reshape;reshape | solution.py:30
  393.6 45.7 %multiply_reduce_fusion = (f32[1600,1024]{1,0:T(8,128)}, f32[1600,1024]{1,0:T(8,128)}) fusion(f32[1600,4,1024]{2,1,0:T(4,128)} %reshape_reshape.3, f32[4]{0:T(128)S(1)} %get-tuple-element.166, f32[4]{0:T(128)S(1)} %get-tuple-element.167), kind=kLoop, calls=%fused_computation.5 | loop fusion | flops 22937600 | bytes 39321632 | tf_op jit(solution)/shard_map/reduce_sum | solution.py:34
  439.2 12.9 %multiply_add_fusion.1 = (f32[1600,1024]{1,0:T(8,128)}, f32[1600,1024]{1,0:T(8,128)}) fusion(f32[1600,1024]{1,0:T(8,128)} %get-tuple-element.133, f32[1600,1024]{1,0:T(8,128)} %get-tuple-element.132, f32[1024]{0:T(1024)S(1)} %get-tuple-element.164, f32[1024]{0:T(1024)S(1)} %get-tuple-element.165), kind=kLoop, calls=%fused_computation.21 | loop fusion | flops 11468800 | bytes 26222592 | tf_op jit(solution)/shard_map/add | solution.py:39
  452.1 48.8 %fusion.13 = bf16[1600,1024]{1,0:T(8,128)(2,1)} fusion(f32[1024,512]{1,0:T(8,128)} %get-tuple-element.169, f32[1024,512]{1,0:T(8,128)} %get-tuple-element.168, f32[1024,512]{1,0:T(8,128)S(1)} %fusion.24, f32[1600,1024]{1,0:T(8,128)} %get-tuple-element.143, f32[1600,1024]{1,0:T(8,128)} %get-tuple-element.142), kind=kOutput, calls=%fused_computation.23 | convolution fusion | flops 40278622208 | bytes 22675456 | tf_op jit(solution)/shard_map/dot_general | solution.py:78
  510.7 13.2 %copy.21 = bf16[64,25,2,512]{0,1,2,3:T(8,128)(2,1)} copy(bf16[64,25,2,512]{3,2,1,0:T(2,128)(2,1)S(1)} %convert_element_type.106) | data formatting | bytes 6553600 | tf_op jit(solution)/shard_map/convert_element_type | solution.py:82
  531.7 23.9 %copy.12 = bf16[2,2,64,25,512]{2,3,1,0,4:T(8,128)(2,1)} copy(bf16[2,2,64,25,512]{4,2,3,1,0:T(8,128)(2,1)} %pad_maximum_fusion) | data formatting | bytes 13107200 | tf_op jit(solution)/shard_map/stack | solution.py:83
  555.6 20.9 %fusion = f32[2,64,1,64,512]{1,3,0,4,2:T(8,128)} fusion(bf16[2,2,64,25,512]{2,3,1,0,4:T(8,128)(2,1)} %copy.12, bf16[64,25,2,512]{0,1,2,3:T(8,128)(2,1)} %copy.21), kind=kOutput, calls=%fused_computation.3 | convolution fusion | flops 423624704 | bytes 26607616 | tf_op jit(solution)/shard_map/opisc,pmsc->oimc/dot_general | solution.py:58
  576.5 63.0 %scatter.4 = f32[2,64,5,64,512]{1,3,0,4,2:T(8,128)} pad(f32[2,64,1,64,512]{1,3,0,4,2:T(8,128)} %fusion, f32[]{:T(128)} %constant.126.clone.1), padding=0_0x0_0x0_4x0_0x0_0 | pad | bytes 100663296 | tf_op jit(solution)/shard_map/scatter | solution.py:85
  639.5 298.8 %while.18 = (s32[]{:T(128)}, bf16[2,64,25,512]{3,1,2,0:T(8,128)(2,1)}, f32[2,64,5,64,512]{1,3,0,4,2:T(8,128)}, bf16[2,2,64,25,512]{2,3,1,0,4:T(8,128)(2,1)}, s32[]{:T(128)}, /*index=5*/s32[]{:T(128)}, s32[]{:T(128)}) while((s32[]{:T(128)}, bf16[2,64,25,512]{3,1,2,0:T(8,128)(2,1)}, f32[2,64,5,64,512]{1,3,0,4,2:T(8,128)}, ...), condition=%wide.region_3.4_spmd, body=%wide.region_2.3_spmd.sunk | while | flops 423624704 | bytes 84934808 | solution.py:94
  642.3 36.5 %collective-permute-done = bf16[2,64,25,512]{3,1,2,0:T(8,128)(2,1)S(1)} collective-permute-done((bf16[2,64,25,512]{3,1,2,0:T(8,128)(2,1)}, bf16[2,64,25,512]{3,1,2,0:T(8,128)(2,1)S(1)}, u32[]{:S(2)}, u32[]{:S(2)}) %collective-permute-start) | collective-permute-done | bytes 3276832 | tf_op jit(solution)/shard_map/while/body/eval_jaxpr/ppermute | solution.py:13
  678.8 12.5 %copy.27 = bf16[2,64,25,512,1]{1,2,0,4,3:T(8,128)(2,1)} copy(bf16[2,64,25,512,1]{3,1,2,0,4:T(8,128)(2,1)S(1)} %bitcast.67) | data formatting | bytes 6553600 | tf_op jit(solution)/shard_map/while/body/eval_jaxpr/ppermute | solution.py:13
  691.2 20.7 %bitcast_dynamic-update-slice_fusion.2 = f32[2,64,5,64,512]{1,3,0,4,2:T(8,128)} fusion(f32[2,64,5,64,512]{1,3,0,4,2:T(8,128)} %get-tuple-element.204, s32[]{:T(128)S(6)} %select_n.82, bf16[2,64,25,512,1]{1,2,0,4,3:T(8,128)(2,1)} %copy.27, bf16[2,2,64,25,512]{2,3,1,0,4:T(8,128)(2,1)} %get-tuple-element.212), kind=kOutput, calls=%fused_computation.clone.1 | convolution fusion | flops 423624704 | bytes 58720260 | tf_op jit(solution)/shard_map/while/body/eval_jaxpr/opisc,pmsc->oimc/dot_general | solution.py:58
  717.1 36.5 %collective-permute-done = bf16[2,64,25,512]{3,1,2,0:T(8,128)(2,1)S(1)} collective-permute-done((bf16[2,64,25,512]{3,1,2,0:T(8,128)(2,1)}, bf16[2,64,25,512]{3,1,2,0:T(8,128)(2,1)S(1)}, u32[]{:S(2)}, u32[]{:S(2)}) %collective-permute-start) | collective-permute-done | bytes 3276832 | tf_op jit(solution)/shard_map/while/body/eval_jaxpr/ppermute | solution.py:13
  753.6 12.5 %copy.27 = bf16[2,64,25,512,1]{1,2,0,4,3:T(8,128)(2,1)} copy(bf16[2,64,25,512,1]{3,1,2,0,4:T(8,128)(2,1)S(1)} %bitcast.67) | data formatting | bytes 6553600 | tf_op jit(solution)/shard_map/while/body/eval_jaxpr/ppermute | solution.py:13
  766.1 20.7 %bitcast_dynamic-update-slice_fusion.2 = f32[2,64,5,64,512]{1,3,0,4,2:T(8,128)} fusion(f32[2,64,5,64,512]{1,3,0,4,2:T(8,128)} %get-tuple-element.204, s32[]{:T(128)S(6)} %select_n.82, bf16[2,64,25,512,1]{1,2,0,4,3:T(8,128)(2,1)} %copy.27, bf16[2,2,64,25,512]{2,3,1,0,4:T(8,128)(2,1)} %get-tuple-element.212), kind=kOutput, calls=%fused_computation.clone.1 | convolution fusion | flops 423624704 | bytes 58720260 | tf_op jit(solution)/shard_map/while/body/eval_jaxpr/opisc,pmsc->oimc/dot_general | solution.py:58
  792.1 36.5 %collective-permute-done = bf16[2,64,25,512]{3,1,2,0:T(8,128)(2,1)S(1)} collective-permute-done((bf16[2,64,25,512]{3,1,2,0:T(8,128)(2,1)}, bf16[2,64,25,512]{3,1,2,0:T(8,128)(2,1)S(1)}, u32[]{:S(2)}, u32[]{:S(2)}) %collective-permute-start) | collective-permute-done | bytes 3276832 | tf_op jit(solution)/shard_map/while/body/eval_jaxpr/ppermute | solution.py:13
  828.6 12.5 %copy.27 = bf16[2,64,25,512,1]{1,2,0,4,3:T(8,128)(2,1)} copy(bf16[2,64,25,512,1]{3,1,2,0,4:T(8,128)(2,1)S(1)} %bitcast.67) | data formatting | bytes 6553600 | tf_op jit(solution)/shard_map/while/body/eval_jaxpr/ppermute | solution.py:13
  841.1 20.6 %bitcast_dynamic-update-slice_fusion.2 = f32[2,64,5,64,512]{1,3,0,4,2:T(8,128)} fusion(f32[2,64,5,64,512]{1,3,0,4,2:T(8,128)} %get-tuple-element.204, s32[]{:T(128)S(6)} %select_n.82, bf16[2,64,25,512,1]{1,2,0,4,3:T(8,128)(2,1)} %copy.27, bf16[2,2,64,25,512]{2,3,1,0,4:T(8,128)(2,1)} %get-tuple-element.212), kind=kOutput, calls=%fused_computation.clone.1 | convolution fusion | flops 423624704 | bytes 58720260 | tf_op jit(solution)/shard_map/while/body/eval_jaxpr/opisc,pmsc->oimc/dot_general | solution.py:58
  867.0 36.5 %collective-permute-done = bf16[2,64,25,512]{3,1,2,0:T(8,128)(2,1)S(1)} collective-permute-done((bf16[2,64,25,512]{3,1,2,0:T(8,128)(2,1)}, bf16[2,64,25,512]{3,1,2,0:T(8,128)(2,1)S(1)}, u32[]{:S(2)}, u32[]{:S(2)}) %collective-permute-start) | collective-permute-done | bytes 3276832 | tf_op jit(solution)/shard_map/while/body/eval_jaxpr/ppermute | solution.py:13
  915.9 20.7 %bitcast_dynamic-update-slice_fusion.2 = f32[2,64,5,64,512]{1,3,0,4,2:T(8,128)} fusion(f32[2,64,5,64,512]{1,3,0,4,2:T(8,128)} %get-tuple-element.204, s32[]{:T(128)S(6)} %select_n.82, bf16[2,64,25,512,1]{1,2,0,4,3:T(8,128)(2,1)} %copy.27, bf16[2,2,64,25,512]{2,3,1,0,4:T(8,128)(2,1)} %get-tuple-element.212), kind=kOutput, calls=%fused_computation.clone.1 | convolution fusion | flops 423624704 | bytes 58720260 | tf_op jit(solution)/shard_map/while/body/eval_jaxpr/opisc,pmsc->oimc/dot_general | solution.py:58
  938.2 124.9 %copy.14 = f32[2,64,5,64,512]{4,3,2,1,0:T(8,128)} copy(f32[2,64,5,64,512]{1,3,0,4,2:T(8,128)} %get-tuple-element.127) | data formatting | bytes 167772160 | tf_op jit(solution)/shard_map/while | solution.py:94
  (21 shorter events, 70.2 us)
Async XLA Ops:
  6.5 198.5 %all-gather.2.cloned.1.call-start = ((), (), s32[]{:S(2)}) async-start(), calls=%async_computation | async-start | bytes 26214400 | tf_op jit(solution)/shard_map/all_gather | solution.py:75
  639.5 39.3 %collective-permute-start = (bf16[2,64,25,512]{3,1,2,0:T(8,128)(2,1)}, bf16[2,64,25,512]{3,1,2,0:T(8,128)(2,1)S(1)}, u32[]{:S(2)}, u32[]{:S(2)}) collective-permute-start(bf16[2,64,25,512]{3,1,2,0:T(8,128)(2,1)} %get-tuple-element.203), channel_id=1, source_target_pairs={{0,7},{1,0},{2,1},{3,2},{4,3},{5,4},{6,5},{7,6},{8,15},{9,8},{10,9... | collective-permute-start | bytes 9830408 | tf_op jit(solution)/shard_map/while/body/eval_jaxpr/ppermute | solution.py:13
  713.5 40.1 %collective-permute-start = (bf16[2,64,25,512]{3,1,2,0:T(8,128)(2,1)}, bf16[2,64,25,512]{3,1,2,0:T(8,128)(2,1)S(1)}, u32[]{:S(2)}, u32[]{:S(2)}) collective-permute-start(bf16[2,64,25,512]{3,1,2,0:T(8,128)(2,1)} %get-tuple-element.203), channel_id=1, source_target_pairs={{0,7},{1,0},{2,1},{3,2},{4,3},{5,4},{6,5},{7,6},{8,15},{9,8},{10,9... | collective-permute-start | bytes 9830408 | tf_op jit(solution)/shard_map/while/body/eval_jaxpr/ppermute | solution.py:13
  788.5 40.1 %collective-permute-start = (bf16[2,64,25,512]{3,1,2,0:T(8,128)(2,1)}, bf16[2,64,25,512]{3,1,2,0:T(8,128)(2,1)S(1)}, u32[]{:S(2)}, u32[]{:S(2)}) collective-permute-start(bf16[2,64,25,512]{3,1,2,0:T(8,128)(2,1)} %get-tuple-element.203), channel_id=1, source_target_pairs={{0,7},{1,0},{2,1},{3,2},{4,3},{5,4},{6,5},{7,6},{8,15},{9,8},{10,9... | collective-permute-start | bytes 9830408 | tf_op jit(solution)/shard_map/while/body/eval_jaxpr/ppermute | solution.py:13
  863.4 40.1 %collective-permute-start = (bf16[2,64,25,512]{3,1,2,0:T(8,128)(2,1)}, bf16[2,64,25,512]{3,1,2,0:T(8,128)(2,1)S(1)}, u32[]{:S(2)}, u32[]{:S(2)}) collective-permute-start(bf16[2,64,25,512]{3,1,2,0:T(8,128)(2,1)} %get-tuple-element.203), channel_id=1, source_target_pairs={{0,7},{1,0},{2,1},{3,2},{4,3},{5,4},{6,5},{7,6},{8,15},{9,8},{10,9... | collective-permute-start | bytes 9830408 | tf_op jit(solution)/shard_map/while/body/eval_jaxpr/ppermute | solution.py:13
Sparse Core Ops, SparseCore 0:
  9.2 195.7 all-gather.1
where the time goes:
time: 1080 us; the launch traced here: 1070 us
  local copies, waits for them, and re-layouts  348 us (32%)
  waiting for transfers between devices  325 us (30%)
  other arithmetic  218 us (20%)
  matrix products  152 us (14%)
  starting transfers between devices  13.6 us (1%)
  between operations  13.6 us (1%)
    all_gather x1, waiting for transfers between devices, shards(): whole_series = lax.all_gather(voltages, 'tm', axis=1, tiled=True)  178 us
    ppermute x4, waiting for transfers between devices, from_behind(): return lax.ppermute(value, axis, pairs)  146 us
    add x1, other arithmetic, polyphase(): filtered + taper[tap_index][None, None, :] * frames[:, tap_index:tap_inde...  134 us
    while x1, local copies, waits for them, and re-layouts, shards(): carried_out = lax.fori_loop(1, lag_count, lag_step, (own_block, visibility))  125 us
    dot_general x5, matrix products, correlate(): jnp.einsum('opisc,pmsc->oimc', conjugated, partner_block, preferred_eleme...  104 us
    scatter x1, local copies, waits for them, and re-layouts, shards(): visibility.at[:, :, 0].set(correlate(conjugated, own_block, spectra_count))  63 us
    ppermute x4, local copies, waits for them, and re-layouts, from_behind(): return lax.ppermute(value, axis, pairs)  49.8 us
    dot_general x1, matrix products, shards(): jnp.dot(twisted, table, precision=lax.Precision.HIGHEST, preferred_elemen...  48.8 us
  transfers between devices with their start and end apart: 5, of which 5 were waited for; matrix products, arithmetic and copies ran while one was open for 2% of the time, Pallas kernels for 0%

commit v1 on v0

--- a/solution.py
+++ b/solution.py
@@ -72,7 +72,21 @@
     spectra_count = NSPEC
     lag_count = stat_count // 2 + 1
     table = dft_table(segment, channel_count, frame_len)
-    whole_series = lax.all_gather(voltages, "tm", axis=1, tiled=True)
+    ways, here, lap = (lax.axis_size("tm"), lax.axis_index("tm"), voltages.shape[1])
+    lengths = [n * ways if d == 1 else n for d, n in enumerate(voltages.shape)]
+    full = lax.dynamic_update_slice_in_dim(
+        jnp.zeros(lengths, voltages.dtype), voltages, here * lap, axis=1
+    )
+    going_up = going_down = voltages
+    for far in range(1, ways // 2 + 1):
+        going_up = lax.ppermute(going_up, "tm", [(d, (d + 1) % ways) for d in range(ways)])
+        full = lax.dynamic_update_slice_in_dim(full, going_up, (here - far) % ways * lap, axis=1)
+        if 2 * far < ways:
+            going_down = lax.ppermute(going_down, "tm", [(d, (d - 1) % ways) for d in range(ways)])
+            full = lax.dynamic_update_slice_in_dim(
+                full, going_down, (here + far) % ways * lap, axis=1
+            )
+    whole_series = full
     filtered = polyphase(whole_series, taper, spectra_count)
     twisted = fold_twiddle(filtered, tm_index, tm_count, frame_len)
     spectra = jnp.dot(

time: 1080 us -> 1220 us (1.13)
  waiting for transfers between devices: 325 us -> 456 us
  other arithmetic: 218 us -> 233 us
  between operations: 13.6 us -> 0.33 us
    ppermute x0 -> x3, waiting for transfers between devices: none -> 310 us  [the longest x2 310 us: shards(): lax.ppermute(going_up, 'tm', [(d, (d + 1) % ways) for d in range(ways)])]
    all_gather x1 -> x0, waiting for transfers between devices: 178 us -> none  [shards(): whole_series = lax.all_gather(voltages, 'tm', axis=1, tiled=True)]
    dynamic_update_slice x0 -> x4, local copies, waits for them, and re-layouts: none -> 13.5 us  [the longest x2 6.75 us: shards(): lax.dynamic_update_slice_in_dim(full, going_up, (here - far) % ways * lap...]
  transfers between devices with their start and end apart: 5 -> 7, of which waited for: 5 -> 6; matrix products, arithmetic and copies ran while one was open for 2% -> 2% of each run, Pallas kernels for 0% -> 0%
where the time goes in v1:
time: 1220 us; the launch traced here: 1210 us
  waiting for transfers between devices  456 us (37%)
  local copies, waits for them, and re-layouts  351 us (29%)
  other arithmetic  233 us (19%)
  matrix products  152 us (12%)
  starting transfers between devices  17.4 us (1%)
    ppermute x2, waiting for transfers between devices, shards(): lax.ppermute(going_up, 'tm', [(d, (d + 1) % ways) for d in range(ways)])  310 us
    ppermute x4, waiting for transfers between devices, from_behind(): return lax.ppermute(value, axis, pairs)  146 us
    add x1, other arithmetic, polyphase(): filtered + taper[tap_index][None, None, :] * frames[:, tap_index:tap_inde...  137 us
    while x1, local copies, waits for them, and re-layouts, shards(): carried_out = lax.fori_loop(1, lag_count, lag_step, (own_block, visibility))  125 us
    dot_general x5, matrix products, correlate(): jnp.einsum('opisc,pmsc->oimc', conjugated, partner_block, preferred_eleme...  104 us
    scatter x1, local copies, waits for them, and re-layouts, shards(): visibility.at[:, :, 0].set(correlate(conjugated, own_block, spectra_count))  63 us
    reduce_sum x1, other arithmetic, fold_twiddle(): sum_imag = -jnp.sum(pieces * jnp.sin(outer_angles)[None, :, None], axis=1)  57.3 us
    ppermute x4, local copies, waits for them, and re-layouts, from_behind(): return lax.ppermute(value, axis, pairs)  49.8 us
  transfers between devices with their start and end apart: 7, of which 6 were waited for; matrix products, arithmetic and copies ran while one was open for 2% of the time, Pallas kernels for 0%

profile of v1, /device:TPU:0, one launch (start us, length us, event | category | flops | bytes accessed | tf_op | source)
XLA Modules:
  0.0 1209.6 jit_solution(11362124293809446201)
XLA Ops:
  26.8 203.0 %collective-permute-done.1 = bf16[64,40960]{1,0:T(8,128)(2,1)} collective-permute-done((bf16[64,40960]{1,0:T(8,128)(2,1)}, bf16[64,40960]{1,0:T(8,128)(2,1)}, u32[]{:S(2)}, u32[]{:S(2)}) %collective-permute-start.1) | collective-permute-done | bytes 5242912 | tf_op jit(solution)/shard_map/ppermute | solution.py:82
  238.1 106.9 %collective-permute-done.3 = bf16[64,40960]{1,0:T(8,128)(2,1)} collective-permute-done((bf16[64,40960]{1,0:T(8,128)(2,1)}, bf16[64,40960]{1,0:T(8,128)(2,1)}, u32[]{:S(2)}, u32[]{:S(2)}) %collective-permute-start.3) | collective-permute-done | bytes 5242912 | tf_op jit(solution)/shard_map/ppermute | solution.py:82
  348.3 13.6 %copy.22 = bf16[8,8,40,4096]{3,2,1,0:T(8,128)(2,1)} copy(bf16[8,8,40,4096]{3,1,2,0:T(8,128)(2,1)S(1)} %bitcast.68) | data formatting | bytes 41943040
  362.0 136.8 %multiply_add_fusion = f32[64,25,4096]{2,1,0:T(8,128)} fusion(bf16[64,40,4096]{2,1,0:T(8,128)(2,1)} %bitcast.66, f32[4096]{0:T(1024)S(1)} %bitcast.83, f32[4096]{0:T(1024)S(1)} %bitcast.84, f32[4096]{0:T(1024)S(1)} %bitcast.70, f32[4096]{0:T(1024)S(1)} %bitcast.71, f32[4096]{0:T(1024)S(1)} %bitcast.72, f32[4096]{0:T(1024)S(1)} %bitcast.73, ...), kind=kLoop, calls=%fused_computation.4 | loop fusion | flops 308019200 | bytes 236191744 | tf_op jit(solution)/shard_map/add | solution.py:51
  498.8 31.4 %reshape_reshape.3 = f32[1600,4,1024]{2,1,0:T(4,128)} reshape(f32[64,25,4096]{2,1,0:T(8,128)} %multiply_add_fusion) | data formatting | bytes 52428800 | tf_op jit(solution)/shard_map/reshape;reshape | solution.py:30
  530.1 57.3 %multiply_reduce_fusion = (f32[1600,1024]{1,0:T(8,128)}, f32[1600,1024]{1,0:T(8,128)}) fusion(f32[1600,4,1024]{2,1,0:T(4,128)} %reshape_reshape.3, f32[4]{0:T(128)S(1)} %get-tuple-element.164, f32[4]{0:T(128)S(1)} %get-tuple-element.165), kind=kLoop, calls=%fused_computation.5 | loop fusion | flops 22937600 | bytes 39321632 | tf_op jit(solution)/shard_map/reduce_sum | solution.py:34
  587.4 13.1 %multiply_add_fusion.1 = (f32[1600,1024]{1,0:T(8,128)}, f32[1600,1024]{1,0:T(8,128)}) fusion(f32[1600,1024]{1,0:T(8,128)} %get-tuple-element.133, f32[1600,1024]{1,0:T(8,128)} %get-tuple-element.132, f32[1024]{0:T(1024)S(1)} %get-tuple-element.166, f32[1024]{0:T(1024)S(1)} %get-tuple-element.167), kind=kLoop, calls=%fused_computation.21 | loop fusion | flops 11468800 | bytes 26222592 | tf_op jit(solution)/shard_map/add | solution.py:39
  600.5 48.5 %fusion.13 = bf16[1600,1024]{1,0:T(8,128)(2,1)} fusion(f32[1024,512]{1,0:T(8,128)} %get-tuple-element.169, f32[1024,512]{1,0:T(8,128)} %get-tuple-element.168, f32[1024,512]{1,0:T(8,128)S(1)} %copy-done, f32[1600,1024]{1,0:T(8,128)} %get-tuple-element.143, f32[1600,1024]{1,0:T(8,128)} %get-tuple-element.142), kind=kOutput, calls=%fused_computation.23 | convolution fusion | flops 40278622208 | bytes 22675456 | tf_op jit(solution)/shard_map/dot_general | solution.py:92
  658.7 13.0 %copy.21 = bf16[64,25,2,512]{0,1,2,3:T(8,128)(2,1)} copy(bf16[64,25,2,512]{3,2,1,0:T(2,128)(2,1)S(1)} %convert_element_type.106) | data formatting | bytes 6553600 | tf_op jit(solution)/shard_map/convert_element_type | solution.py:96
  679.5 23.9 %copy.12 = bf16[2,2,64,25,512]{2,3,1,0,4:T(8,128)(2,1)} copy(bf16[2,2,64,25,512]{4,2,3,1,0:T(8,128)(2,1)} %pad_maximum_fusion) | data formatting | bytes 13107200 | tf_op jit(solution)/shard_map/stack | solution.py:97
  703.4 20.9 %fusion = f32[2,64,1,64,512]{1,3,0,4,2:T(8,128)} fusion(bf16[2,2,64,25,512]{2,3,1,0,4:T(8,128)(2,1)} %copy.12, bf16[64,25,2,512]{0,1,2,3:T(8,128)(2,1)} %copy.21), kind=kOutput, calls=%fused_computation.3 | convolution fusion | flops 423624704 | bytes 26607616 | tf_op jit(solution)/shard_map/opisc,pmsc->oimc/dot_general | solution.py:58
  724.3 63.0 %scatter.4 = f32[2,64,5,64,512]{1,3,0,4,2:T(8,128)} pad(f32[2,64,1,64,512]{1,3,0,4,2:T(8,128)} %fusion, f32[]{:T(128)} %constant.152.clone.1), padding=0_0x0_0x0_4x0_0x0_0 | pad | bytes 100663296 | tf_op jit(solution)/shard_map/scatter | solution.py:99
  787.3 297.2 %while.18 = (s32[]{:T(128)}, bf16[2,64,25,512]{3,1,2,0:T(8,128)(2,1)}, f32[2,64,5,64,512]{1,3,0,4,2:T(8,128)}, bf16[2,2,64,25,512]{2,3,1,0,4:T(8,128)(2,1)}, s32[]{:T(128)}, /*index=5*/s32[]{:T(128)}, s32[]{:T(128)}) while((s32[]{:T(128)}, bf16[2,64,25,512]{3,1,2,0:T(8,128)(2,1)}, f32[2,64,5,64,512]{1,3,0,4,2:T(8,128)}, ...), condition=%wide.region_3.4_spmd, body=%wide.region_2.3_spmd.sunk | while | flops 423624704 | bytes 84934808 | solution.py:108
  788.5 36.5 %collective-permute-done = bf16[2,64,25,512]{3,1,2,0:T(8,128)(2,1)S(1)} collective-permute-done((bf16[2,64,25,512]{3,1,2,0:T(8,128)(2,1)}, bf16[2,64,25,512]{3,1,2,0:T(8,128)(2,1)S(1)}, u32[]{:S(2)}, u32[]{:S(2)}) %collective-permute-start) | collective-permute-done | bytes 3276832 | tf_op jit(solution)/shard_map/while/body/eval_jaxpr/ppermute | solution.py:13
  837.5 20.6 %bitcast_dynamic-update-slice_fusion.2 = f32[2,64,5,64,512]{1,3,0,4,2:T(8,128)} fusion(f32[2,64,5,64,512]{1,3,0,4,2:T(8,128)} %get-tuple-element.204, s32[]{:T(128)S(6)} %select_n.115, bf16[2,64,25,512,1]{1,2,0,4,3:T(8,128)(2,1)} %copy.27, bf16[2,2,64,25,512]{2,3,1,0,4:T(8,128)(2,1)} %get-tuple-element.212), kind=kOutput, calls=%fused_computation.clone.1 | convolution fusion | flops 423624704 | bytes 58720260 | tf_op jit(solution)/shard_map/while/body/eval_jaxpr/opisc,pmsc->oimc/dot_general | solution.py:58
  863.4 36.5 %collective-permute-done = bf16[2,64,25,512]{3,1,2,0:T(8,128)(2,1)S(1)} collective-permute-done((bf16[2,64,25,512]{3,1,2,0:T(8,128)(2,1)}, bf16[2,64,25,512]{3,1,2,0:T(8,128)(2,1)S(1)}, u32[]{:S(2)}, u32[]{:S(2)}) %collective-permute-start) | collective-permute-done | bytes 3276832 | tf_op jit(solution)/shard_map/while/body/eval_jaxpr/ppermute | solution.py:13
  899.9 12.5 %copy.27 = bf16[2,64,25,512,1]{1,2,0,4,3:T(8,128)(2,1)} copy(bf16[2,64,25,512,1]{3,1,2,0,4:T(8,128)(2,1)S(1)} %bitcast.67) | data formatting | bytes 6553600 | tf_op jit(solution)/shard_map/while/body/eval_jaxpr/ppermute | solution.py:13
  912.4 20.8 %bitcast_dynamic-update-slice_fusion.2 = f32[2,64,5,64,512]{1,3,0,4,2:T(8,128)} fusion(f32[2,64,5,64,512]{1,3,0,4,2:T(8,128)} %get-tuple-element.204, s32[]{:T(128)S(6)} %select_n.115, bf16[2,64,25,512,1]{1,2,0,4,3:T(8,128)(2,1)} %copy.27, bf16[2,2,64,25,512]{2,3,1,0,4:T(8,128)(2,1)} %get-tuple-element.212), kind=kOutput, calls=%fused_computation.clone.1 | convolution fusion | flops 423624704 | bytes 58720260 | tf_op jit(solution)/shard_map/while/body/eval_jaxpr/opisc,pmsc->oimc/dot_general | solution.py:58
  938.4 36.5 %collective-permute-done = bf16[2,64,25,512]{3,1,2,0:T(8,128)(2,1)S(1)} collective-permute-done((bf16[2,64,25,512]{3,1,2,0:T(8,128)(2,1)}, bf16[2,64,25,512]{3,1,2,0:T(8,128)(2,1)S(1)}, u32[]{:S(2)}, u32[]{:S(2)}) %collective-permute-start) | collective-permute-done | bytes 3276832 | tf_op jit(solution)/shard_map/while/body/eval_jaxpr/ppermute | solution.py:13
  974.9 12.5 %copy.27 = bf16[2,64,25,512,1]{1,2,0,4,3:T(8,128)(2,1)} copy(bf16[2,64,25,512,1]{3,1,2,0,4:T(8,128)(2,1)S(1)} %bitcast.67) | data formatting | bytes 6553600 | tf_op jit(solution)/shard_map/while/body/eval_jaxpr/ppermute | solution.py:13
  987.3 20.6 %bitcast_dynamic-update-slice_fusion.2 = f32[2,64,5,64,512]{1,3,0,4,2:T(8,128)} fusion(f32[2,64,5,64,512]{1,3,0,4,2:T(8,128)} %get-tuple-element.204, s32[]{:T(128)S(6)} %select_n.115, bf16[2,64,25,512,1]{1,2,0,4,3:T(8,128)(2,1)} %copy.27, bf16[2,2,64,25,512]{2,3,1,0,4:T(8,128)(2,1)} %get-tuple-element.212), kind=kOutput, calls=%fused_computation.clone.1 | convolution fusion | flops 423624704 | bytes 58720260 | tf_op jit(solution)/shard_map/while/body/eval_jaxpr/opisc,pmsc->oimc/dot_general | solution.py:58
  1013.2 36.5 %collective-permute-done = bf16[2,64,25,512]{3,1,2,0:T(8,128)(2,1)S(1)} collective-permute-done((bf16[2,64,25,512]{3,1,2,0:T(8,128)(2,1)}, bf16[2,64,25,512]{3,1,2,0:T(8,128)(2,1)S(1)}, u32[]{:S(2)}, u32[]{:S(2)}) %collective-permute-start) | collective-permute-done | bytes 3276832 | tf_op jit(solution)/shard_map/while/body/eval_jaxpr/ppermute | solution.py:13
  1062.2 20.7 %bitcast_dynamic-update-slice_fusion.2 = f32[2,64,5,64,512]{1,3,0,4,2:T(8,128)} fusion(f32[2,64,5,64,512]{1,3,0,4,2:T(8,128)} %get-tuple-element.204, s32[]{:T(128)S(6)} %select_n.115, bf16[2,64,25,512,1]{1,2,0,4,3:T(8,128)(2,1)} %copy.27, bf16[2,2,64,25,512]{2,3,1,0,4:T(8,128)(2,1)} %get-tuple-element.212), kind=kOutput, calls=%fused_computation.clone.1 | convolution fusion | flops 423624704 | bytes 58720260 | tf_op jit(solution)/shard_map/while/body/eval_jaxpr/opisc,pmsc->oimc/dot_general | solution.py:58
  1084.5 124.9 %copy.14 = f32[2,64,5,64,512]{4,3,2,1,0:T(8,128)} copy(f32[2,64,5,64,512]{1,3,0,4,2:T(8,128)} %get-tuple-element.127) | data formatting | bytes 167772160 | tf_op jit(solution)/shard_map/while | solution.py:108
  (33 shorter events, 99.4 us)
Async XLA Ops:
  0.0 234.7 %collective-permute-start.2 = (bf16[64,40960]{1,0:T(8,128)(2,1)}, bf16[64,40960]{1,0:T(8,128)(2,1)}, u32[]{:S(2)}, u32[]{:S(2)}) collective-permute-start(bf16[64,40960]{1,0:T(8,128)(2,1)} %param.6), channel_id=1, source_target_pairs={{0,24},{8,0},{16,8},{24,16},{1,25},{9,1},{17,9},{25,17},{2,26},{10... | collective-permute-start | bytes 15728648 | tf_op jit(solution)/shard_map/ppermute | solution.py:85
  3.9 226.0 %collective-permute-start.1 = (bf16[64,40960]{1,0:T(8,128)(2,1)}, bf16[64,40960]{1,0:T(8,128)(2,1)}, u32[]{:S(2)}, u32[]{:S(2)}) collective-permute-start(bf16[64,40960]{1,0:T(8,128)(2,1)} %param.6), channel_id=1, source_target_pairs={{0,8},{8,16},{16,24},{24,0},{1,9},{9,17},{17,25},{25,1},{2,10},{10... | collective-permute-start | bytes 15728648 | tf_op jit(solution)/shard_map/ppermute | solution.py:82
  21.7 4.9 copy-start.1
  229.9 115.1 %collective-permute-start.3 = (bf16[64,40960]{1,0:T(8,128)(2,1)}, bf16[64,40960]{1,0:T(8,128)(2,1)}, u32[]{:S(2)}, u32[]{:S(2)}) collective-permute-start(bf16[64,40960]{1,0:T(8,128)(2,1)} %collective-permute-done.1), channel_id=1, source_target_pairs={{0,8},{8,16},{16,24},{24,0},{1,9},{9,17},{17,25},{25,1},{2,10},{10... | collective-permute-start | bytes 15728648 | tf_op jit(solution)/shard_map/ppermute | solution.py:82
  587.4 13.1 %copy-start = (f32[1024,512]{1,0:T(8,128)S(1)}, f32[1024,512]{1,0:T(8,128)}, u32[]{:S(2)}) copy-start(f32[1024,512]{1,0:T(8,128)} %fusion.24) | copy-start | bytes 6291460
  787.3 37.8 %collective-permute-start = (bf16[2,64,25,512]{3,1,2,0:T(8,128)(2,1)}, bf16[2,64,25,512]{3,1,2,0:T(8,128)(2,1)S(1)}, u32[]{:S(2)}, u32[]{:S(2)}) collective-permute-start(bf16[2,64,25,512]{3,1,2,0:T(8,128)(2,1)} %get-tuple-element.203), channel_id=1, source_target_pairs={{0,7},{1,0},{2,1},{3,2},{4,3},{5,4},{6,5},{7,6},{8,15},{9,8},{10,9... | collective-permute-start | bytes 9830408 | tf_op jit(solution)/shard_map/while/body/eval_jaxpr/ppermute | solution.py:13
  859.8 40.1 %collective-permute-start = (bf16[2,64,25,512]{3,1,2,0:T(8,128)(2,1)}, bf16[2,64,25,512]{3,1,2,0:T(8,128)(2,1)S(1)}, u32[]{:S(2)}, u32[]{:S(2)}) collective-permute-start(bf16[2,64,25,512]{3,1,2,0:T(8,128)(2,1)} %get-tuple-element.203), channel_id=1, source_target_pairs={{0,7},{1,0},{2,1},{3,2},{4,3},{5,4},{6,5},{7,6},{8,15},{9,8},{10,9... | collective-permute-start | bytes 9830408 | tf_op jit(solution)/shard_map/while/body/eval_jaxpr/ppermute | solution.py:13
  934.8 40.1 %collective-permute-start = (bf16[2,64,25,512]{3,1,2,0:T(8,128)(2,1)}, bf16[2,64,25,512]{3,1,2,0:T(8,128)(2,1)S(1)}, u32[]{:S(2)}, u32[]{:S(2)}) collective-permute-start(bf16[2,64,25,512]{3,1,2,0:T(8,128)(2,1)} %get-tuple-element.203), channel_id=1, source_target_pairs={{0,7},{1,0},{2,1},{3,2},{4,3},{5,4},{6,5},{7,6},{8,15},{9,8},{10,9... | collective-permute-start | bytes 9830408 | tf_op jit(solution)/shard_map/while/body/eval_jaxpr/ppermute | solution.py:13
  1009.6 40.1 %collective-permute-start = (bf16[2,64,25,512]{3,1,2,0:T(8,128)(2,1)}, bf16[2,64,25,512]{3,1,2,0:T(8,128)(2,1)S(1)}, u32[]{:S(2)}, u32[]{:S(2)}) collective-permute-start(bf16[2,64,25,512]{3,1,2,0:T(8,128)(2,1)} %get-tuple-element.203), channel_id=1, source_target_pairs={{0,7},{1,0},{2,1},{3,2},{4,3},{5,4},{6,5},{7,6},{8,15},{9,8},{10,9... | collective-permute-start | bytes 9830408 | tf_op jit(solution)/shard_map/while/body/eval_jaxpr/ppermute | solution.py:13
